TPU v7x, 32 devices: a whole 2x2x4 slice. The times are simulated.
32 devices in a mesh: dp: 4 (over z), expert: 8 (over y, x, core).
Axes of the slice: x: 2, y: 2, z: 4, core: 2. Of those that a mesh axis runs over, the one named last changes fastest.
Arguments:
- tokens: bfloat16 [128, 144, 512], P(('dp', 'expert')), may hold values from -6 to 6
- patch_counts: int32 [128], P(('dp', 'expert')), may hold values from 49 to 144, as said below
- expert_ids: int32 [128, 144, 2], P(('dp', 'expert')), may hold values from 0 to 7, all different within a row
- priority: int32 [32, 576], P(('dp', 'expert')), may hold values from 0 to 575, each once within a row
- out_grad: bfloat16 [128, 144, 512], P(('dp', 'expert')), may hold values from -6 to 6
- first_gain: bfloat16 [512], P(('dp', 'expert')), may hold values from 0.5 to 1.5
- first_shift: bfloat16 [512], P(('dp', 'expert')), may hold values from -1.25 to 1.25
- qkv_weight: bfloat16 [512, 1536], P(('dp', 'expert')), may hold values from -0.25 to 0.25
- query_bias: bfloat16 [512], P(('dp', 'expert')), may hold values from -1.75 to 1.75
- value_bias: bfloat16 [512], P(('dp', 'expert')), may hold values from -1.75 to 1.75
- proj_weight: bfloat16 [512, 512], P(('dp', 'expert')), may hold values from -2 to 2
- proj_bias: bfloat16 [512], P(('dp', 'expert')), may hold values from -1.75 to 1.75
- second_gain: bfloat16 [512], P(('dp', 'expert')), may hold values from 0.5 to 1.5
- second_shift: bfloat16 [512], P(('dp', 'expert')), may hold values from -1.25 to 1.25
- router_weight: bfloat16 [512, 8], P(('dp', 'expert')), may hold values from -0.1875 to 0.1875
- hidden_weight: bfloat16 [8, 2048, 512], P('expert', 'dp'), may hold values from -0.25 to 0.25
- hidden_bias: bfloat16 [8, 2048], P('expert', 'dp'), may hold values from -1.25 to 1.25
- return_weight: bfloat16 [8, 2048, 512], P('expert', 'dp'), may hold values from -0.875 to 0.875
- return_bias: bfloat16 [8, 512], P('expert', 'dp'), may hold values from -6 to 6
Outputs:
- block_out: bfloat16 [128, 144, 512], P(('dp', 'expert'))
- tokens_grad: bfloat16 [128, 144, 512], P(('dp', 'expert'))
- first_gain_grad: float32 [512], P(('dp', 'expert'))
- first_shift_grad: float32 [512], P(('dp', 'expert'))
- qkv_weight_grad: float32 [512, 1536], P(('dp', 'expert'))
- query_bias_grad: float32 [512], P(('dp', 'expert'))
- value_bias_grad: float32 [512], P(('dp', 'expert'))
- proj_weight_grad: float32 [512, 512], P(('dp', 'expert'))
- proj_bias_grad: float32 [512], P(('dp', 'expert'))
- second_gain_grad: float32 [512], P(('dp', 'expert'))
- second_shift_grad: float32 [512], P(('dp', 'expert'))
- router_weight_grad: float32 [512, 8], P(('dp', 'expert'))
- hidden_weight_grad: float32 [8, 2048, 512], P('expert', 'dp')
- hidden_bias_grad: float32 [8, 2048], P('expert', 'dp')
- return_weight_grad: float32 [8, 2048, 512], P('expert', 'dp')
- return_bias_grad: float32 [8, 512], P('expert', 'dp')
Inputs may be any that keep to these rules, and one draw needn't show every extreme that they name: Image i has its patches at its first patch_counts[i] positions and padding after them; every count is 49 or 144. `expert_ids`: the 2 experts of a position differ. `priority`: each row is a permutation of the ranks 0 to 575 of its group's positions.
All inputs are finite; a program needn't handle non-finite values.
Results may differ from a plain program's by a relative error of at most 0.017.
Values may be sent and summed in bfloat16 or wider, within the bound.
No kernel may reach another device: no remote copies, remote signals or barrier semaphores. Data moves between devices by JAX's collectives and lax.ppermute only.
A program may use at most 128 MiB of HBM per device.

v0:
```python
import math

import jax
import jax.numpy as jnp
from jax import lax
from jax.sharding import PartitionSpec as P

HEADS = 8


norm_eps = 1e-06
neg_large = -1e30


def layer_norm(values, norm_gain, norm_shift):
    center = values - jnp.mean(values, axis=-1, keepdims=True)
    spread = jnp.mean(center * center, axis=-1, keepdims=True)
    return center * lax.rsqrt(spread + norm_eps) * norm_gain + norm_shift


def router_softmax(logits):
    highest = jnp.max(logits, axis=-1, keepdims=True)
    raised = jnp.exp(logits - highest)
    return raised / jnp.sum(raised, axis=-1, keepdims=True)


def gelu_tanh(values):
    return jax.nn.gelu(values, approximate=True)


def route_group(choices, valid_rows, rank_rows, experts_all, capacity):
    tok_count = choices.shape[0]
    top_count = choices.shape[1]
    expert_iota = jnp.arange(experts_all, dtype=jnp.int32)
    onehot = (
        (choices[:, :, None] == expert_iota[None, None, :]) & valid_rows[:, None, None]
    ).astype(jnp.int32)
    order_key = (
        jnp.arange(top_count, dtype=jnp.int32)[None, :] * tok_count + rank_rows[:, None]
    ).reshape(-1)
    ordered = (
        jnp.zeros((top_count * tok_count, experts_all), jnp.int32)
        .at[order_key]
        .set(onehot.reshape(-1, experts_all))
    )
    earlier = jnp.cumsum(ordered, axis=0) - ordered
    slot_index = jnp.sum(
        earlier[order_key].reshape(tok_count, top_count, experts_all) * onehot, axis=-1
    )
    is_kept = valid_rows[:, None] & (slot_index < capacity)
    return (slot_index, is_kept)


def make_table(choices, slot_index, is_kept, experts_all, capacity):
    tok_count = choices.shape[0]
    flat_index = jnp.where(
        is_kept, choices * capacity + slot_index, experts_all * capacity
    ).reshape(-1)
    owners = jnp.broadcast_to(
        jnp.arange(tok_count, dtype=jnp.int32)[:, None], choices.shape
    ).reshape(-1)
    token_table = (
        jnp.full((experts_all * capacity,), tok_count, jnp.int32)
        .at[flat_index]
        .set(owners, mode="drop")
    )
    return (token_table, flat_index)


def attention_scores(query_low, key_low, key_valid, scale_factor):
    scores = (
        jnp.einsum("bqhd,bkhd->bhqk", query_low, key_low, preferred_element_type=jnp.float32)
        * scale_factor
    )
    return jnp.where(key_valid[:, None, None, :], scores, neg_large)


def on_device(
    tokens,
    patch_counts,
    expert_ids,
    priority,
    out_grad,
    first_gain,
    first_shift,
    qkv_weight,
    query_bias,
    value_bias,
    proj_weight,
    proj_bias,
    second_gain,
    second_shift,
    router_weight,
    hidden_weight,
    hidden_bias,
    return_weight,
    return_bias,
):
    images = tokens.shape[0]
    patches = tokens.shape[1]
    model_width = tokens.shape[2]
    tok_count = images * patches
    top_count = expert_ids.shape[2]
    experts_all = router_weight.shape[1]
    local_experts = hidden_weight.shape[0]
    capacity = (tok_count * top_count * 105 + 100 * experts_all - 1) // (100 * experts_all)
    head_count = HEADS
    head_size = model_width // head_count
    scale_factor = 1.0 / math.sqrt(head_size)
    split_shape = (images, patches, head_count, head_size)
    (
        gain_one,
        shift_one,
        qkv_full,
        query_add,
        value_add,
        proj_full,
        proj_add,
        gain_two,
        shift_two,
        router_full,
    ) = (
        lax.all_gather(first_gain, ("dp", "expert"), axis=0, tiled=True),
        lax.all_gather(first_shift, ("dp", "expert"), axis=0, tiled=True),
        lax.all_gather(qkv_weight, ("dp", "expert"), axis=0, tiled=True),
        lax.all_gather(query_bias, ("dp", "expert"), axis=0, tiled=True),
        lax.all_gather(value_bias, ("dp", "expert"), axis=0, tiled=True),
        lax.all_gather(proj_weight, ("dp", "expert"), axis=0, tiled=True),
        lax.all_gather(proj_bias, ("dp", "expert"), axis=0, tiled=True),
        lax.all_gather(second_gain, ("dp", "expert"), axis=0, tiled=True),
        lax.all_gather(second_shift, ("dp", "expert"), axis=0, tiled=True),
        lax.all_gather(router_weight, ("dp", "expert"), axis=0, tiled=True),
    )
    residual_in = tokens.astype(jnp.float32)
    key_valid = lax.broadcasted_iota(jnp.int32, (images, patches), 1) < patch_counts[:, None]
    first_low = (
        layer_norm(residual_in, gain_one.astype(jnp.float32), shift_one.astype(jnp.float32))
        .astype(jnp.bfloat16)
        .reshape(tok_count, model_width)
    )
    qkv_out = jnp.dot(first_low, qkv_full, preferred_element_type=jnp.float32)
    query_low = (
        (qkv_out[:, :model_width] + query_add.astype(jnp.float32))
        .astype(jnp.bfloat16)
        .reshape(split_shape)
    )
    key_low = qkv_out[:, model_width : 2 * model_width].astype(jnp.bfloat16).reshape(split_shape)
    value_low = (
        (qkv_out[:, 2 * model_width :] + value_add.astype(jnp.float32))
        .astype(jnp.bfloat16)
        .reshape(split_shape)
    )
    masked = attention_scores(query_low, key_low, key_valid, scale_factor)
    highest = jnp.max(masked, axis=-1, keepdims=True)
    raised = jnp.exp(masked - highest)
    row_total = jnp.sum(raised, axis=-1, keepdims=True)
    probs_low = (raised / row_total).astype(jnp.bfloat16)
    log_total = highest + jnp.log(row_total)
    context = (
        jnp.einsum("bhqk,bkhd->bqhd", probs_low, value_low, preferred_element_type=jnp.float32)
        .astype(jnp.bfloat16)
        .reshape(tok_count, model_width)
    )
    hidden_res = (
        residual_in.reshape(tok_count, model_width)
        + jnp.dot(context, proj_full, preferred_element_type=jnp.float32)
        + proj_add.astype(jnp.float32)
    )
    second_low = layer_norm(
        hidden_res, gain_two.astype(jnp.float32), shift_two.astype(jnp.float32)
    ).astype(jnp.bfloat16)
    logits = jnp.dot(second_low, router_full, preferred_element_type=jnp.float32)
    router_probs = router_softmax(logits)
    choices = expert_ids.reshape(tok_count, top_count)
    valid_rows = key_valid.reshape(tok_count)
    slot_index, is_kept = route_group(choices, valid_rows, priority[0], experts_all, capacity)
    token_table, flat_index = make_table(choices, slot_index, is_kept, experts_all, capacity)
    choice_hot = (
        choices[:, :, None] == jnp.arange(experts_all, dtype=jnp.int32)[None, None, :]
    ).astype(jnp.float32)
    kept_float = is_kept.astype(jnp.float32)
    gate_weights = jnp.sum(router_probs[:, None, :] * choice_hot, axis=-1) * kept_float
    positions = choices * capacity + jnp.minimum(slot_index, capacity - 1)
    padded_second = jnp.concatenate([second_low, jnp.zeros((1, model_width), jnp.bfloat16)], axis=0)
    dispatch = padded_second[token_table].reshape(experts_all, capacity, model_width)
    arrived = lax.all_to_all(dispatch, "expert", split_axis=0, concat_axis=0, tiled=True).reshape(
        -1, local_experts, capacity, model_width
    )
    in_full, in_add, out_full, out_add = (
        lax.all_gather(hidden_weight, "dp", axis=1, tiled=True),
        lax.all_gather(hidden_bias, "dp", axis=1, tiled=True),
        lax.all_gather(return_weight, "dp", axis=1, tiled=True),
        lax.all_gather(return_bias, "dp", axis=1, tiled=True),
    )
    pre_act = (
        jnp.einsum("sjcd,jfd->sjcf", arrived, in_full, preferred_element_type=jnp.float32)
        + in_add.astype(jnp.float32)[None, :, None, :]
    )
    act_low = gelu_tanh(pre_act).astype(jnp.bfloat16)
    expert_out = (
        jnp.einsum("sjcf,jfd->sjcd", act_low, out_full, preferred_element_type=jnp.float32)
        + out_add.astype(jnp.float32)[None, :, None, :]
    ).astype(jnp.bfloat16)
    returned = lax.all_to_all(
        expert_out.reshape(experts_all, capacity, model_width),
        "expert",
        split_axis=0,
        concat_axis=0,
        tiled=True,
    )
    picked = returned.reshape(experts_all * capacity, model_width)[positions].astype(jnp.float32)
    block_out = (
        (hidden_res + jnp.sum(gate_weights[:, :, None] * picked, axis=1))
        .astype(jnp.bfloat16)
        .reshape(images, patches, model_width)
    )
    (
        back_gain_one,
        back_shift_one,
        back_qkv,
        back_query,
        back_value,
        back_proj,
        back_proj_add,
        back_gain_two,
        back_shift_two,
        back_router,
    ) = (
        lax.all_gather(first_gain, ("dp", "expert"), axis=0, tiled=True),
        lax.all_gather(first_shift, ("dp", "expert"), axis=0, tiled=True),
        lax.all_gather(qkv_weight, ("dp", "expert"), axis=0, tiled=True),
        lax.all_gather(query_bias, ("dp", "expert"), axis=0, tiled=True),
        lax.all_gather(value_bias, ("dp", "expert"), axis=0, tiled=True),
        lax.all_gather(proj_weight, ("dp", "expert"), axis=0, tiled=True),
        lax.all_gather(proj_bias, ("dp", "expert"), axis=0, tiled=True),
        lax.all_gather(second_gain, ("dp", "expert"), axis=0, tiled=True),
        lax.all_gather(second_shift, ("dp", "expert"), axis=0, tiled=True),
        lax.all_gather(router_weight, ("dp", "expert"), axis=0, tiled=True),
    )
    back_in, back_in_add, back_out, back_out_add = (
        lax.all_gather(hidden_weight, "dp", axis=1, tiled=True),
        lax.all_gather(hidden_bias, "dp", axis=1, tiled=True),
        lax.all_gather(return_weight, "dp", axis=1, tiled=True),
        lax.all_gather(return_bias, "dp", axis=1, tiled=True),
    )
    upstream = out_grad.astype(jnp.float32).reshape(tok_count, model_width)
    gate_grad = jnp.sum(upstream[:, None, :] * picked, axis=-1) * kept_float
    prob_grad = jnp.sum(gate_grad[:, :, None] * choice_hot, axis=1)
    unused_probs, soft_back = jax.vjp(router_softmax, logits)
    logit_low = soft_back(prob_grad)[0].astype(jnp.bfloat16)
    router_grad = jnp.einsum("td,te->de", second_low, logit_low, preferred_element_type=jnp.float32)
    weight_table = (
        jnp.zeros((experts_all * capacity,), jnp.float32)
        .at[flat_index]
        .set(gate_weights.reshape(-1), mode="drop")
    )
    padded_up = jnp.concatenate([upstream, jnp.zeros((1, model_width), jnp.float32)], axis=0)
    slot_grad = (
        (padded_up[token_table] * weight_table[:, None])
        .astype(jnp.bfloat16)
        .reshape(experts_all, capacity, model_width)
    )
    grad_arrived = lax.all_to_all(
        slot_grad, "expert", split_axis=0, concat_axis=0, tiled=True
    ).reshape(-1, local_experts, capacity, model_width)
    act_grad = jnp.einsum(
        "sjcd,jfd->sjcf", grad_arrived, back_out, preferred_element_type=jnp.float32
    )
    unused_act, gelu_back = jax.vjp(gelu_tanh, pre_act)
    pre_grad = gelu_back(act_grad)[0].astype(jnp.bfloat16)
    slot_input_grad = (
        jnp.einsum("sjcf,jfd->sjcd", pre_grad, back_in, preferred_element_type=jnp.float32)
        .astype(jnp.bfloat16)
        .reshape(experts_all, capacity, model_width)
    )
    dispatch_back = lax.all_to_all(
        slot_input_grad, "expert", split_axis=0, concat_axis=0, tiled=True
    ).reshape(experts_all * capacity, model_width)
    return_w_grad = jnp.einsum(
        "sjcf,sjcd->jfd", act_low, grad_arrived, preferred_element_type=jnp.float32
    )
    return_b_grad = jnp.sum(grad_arrived.astype(jnp.float32), axis=(0, 2))
    hidden_w_grad = jnp.einsum(
        "sjcf,sjcd->jfd", pre_grad, arrived, preferred_element_type=jnp.float32
    )
    hidden_b_grad = jnp.sum(pre_grad.astype(jnp.float32), axis=(0, 2))
    hidden_w_sum, hidden_b_sum, return_w_sum, return_b_sum = (
        lax.psum_scatter(
            hidden_w_grad.astype(jnp.bfloat16), "dp", scatter_dimension=1, tiled=True
        ).astype(jnp.float32),
        lax.psum_scatter(
            hidden_b_grad.astype(jnp.bfloat16), "dp", scatter_dimension=1, tiled=True
        ).astype(jnp.float32),
        lax.psum_scatter(
            return_w_grad.astype(jnp.bfloat16), "dp", scatter_dimension=1, tiled=True
        ).astype(jnp.float32),
        lax.psum_scatter(
            return_b_grad.astype(jnp.bfloat16), "dp", scatter_dimension=1, tiled=True
        ).astype(jnp.float32),
    )
    second_grad = jnp.einsum(
        "te,de->td", logit_low, back_router, preferred_element_type=jnp.float32
    )
    second_grad = second_grad + jnp.sum(
        kept_float[:, :, None] * dispatch_back[positions].astype(jnp.float32), axis=1
    )
    unused_norm, norm_back = jax.vjp(
        layer_norm,
        hidden_res,
        back_gain_two.astype(jnp.float32),
        back_shift_two.astype(jnp.float32),
    )
    through_norm, gain_two_grad, shift_two_grad = norm_back(second_grad)
    residual_grad = upstream + through_norm
    proj_in = residual_grad.astype(jnp.bfloat16)
    proj_w_grad = jnp.einsum("td,te->de", context, proj_in, preferred_element_type=jnp.float32)
    proj_b_grad = jnp.sum(proj_in.astype(jnp.float32), axis=0)
    context_grad = (
        jnp.einsum("te,de->td", proj_in, back_proj, preferred_element_type=jnp.float32)
        .astype(jnp.bfloat16)
        .reshape(split_shape)
    )
    scores_again = attention_scores(query_low, key_low, key_valid, scale_factor)
    probs_again = jnp.exp(scores_again - log_total)
    probs_again_low = probs_again.astype(jnp.bfloat16)
    weight_grad = jnp.einsum(
        "bqhd,bkhd->bhqk", context_grad, value_low, preferred_element_type=jnp.float32
    )
    value_grad = jnp.einsum(
        "bhqk,bqhd->bkhd", probs_again_low, context_grad, preferred_element_type=jnp.float32
    ).astype(jnp.bfloat16)
    score_grad = (
        probs_again * (weight_grad - jnp.sum(weight_grad * probs_again, axis=-1, keepdims=True))
    ).astype(jnp.bfloat16)
    query_grad = (
        jnp.einsum("bhqk,bkhd->bqhd", score_grad, key_low, preferred_element_type=jnp.float32)
        * scale_factor
    ).astype(jnp.bfloat16)
    key_grad = (
        jnp.einsum("bhqk,bqhd->bkhd", score_grad, query_low, preferred_element_type=jnp.float32)
        * scale_factor
    ).astype(jnp.bfloat16)
    query_flat = query_grad.reshape(tok_count, model_width)
    value_flat = value_grad.reshape(tok_count, model_width)
    qkv_grad = jnp.concatenate(
        [query_flat, key_grad.reshape(tok_count, model_width), value_flat], axis=1
    )
    qkv_w_grad = jnp.einsum("td,te->de", first_low, qkv_grad, preferred_element_type=jnp.float32)
    query_b_grad = jnp.sum(query_flat.astype(jnp.float32), axis=0)
    value_b_grad = jnp.sum(value_flat.astype(jnp.float32), axis=0)
    first_grad = jnp.einsum(
        "te,de->td", qkv_grad, back_qkv, preferred_element_type=jnp.float32
    ).reshape(images, patches, model_width)
    unused_first, first_back = jax.vjp(
        layer_norm,
        residual_in,
        back_gain_one.astype(jnp.float32),
        back_shift_one.astype(jnp.float32),
    )
    through_first, gain_one_grad, shift_one_grad = first_back(first_grad)
    tokens_grad = (residual_grad.reshape(images, patches, model_width) + through_first).astype(
        jnp.bfloat16
    )
    (
        gain_one_sum,
        shift_one_sum,
        qkv_sum,
        query_sum,
        value_sum,
        proj_sum,
        proj_add_sum,
        gain_two_sum,
        shift_two_sum,
        router_sum,
    ) = (
        lax.psum_scatter(gain_one_grad, ("dp", "expert"), scatter_dimension=0, tiled=True),
        lax.psum_scatter(shift_one_grad, ("dp", "expert"), scatter_dimension=0, tiled=True),
        lax.psum_scatter(qkv_w_grad, ("dp", "expert"), scatter_dimension=0, tiled=True),
        lax.psum_scatter(query_b_grad, ("dp", "expert"), scatter_dimension=0, tiled=True),
        lax.psum_scatter(value_b_grad, ("dp", "expert"), scatter_dimension=0, tiled=True),
        lax.psum_scatter(proj_w_grad, ("dp", "expert"), scatter_dimension=0, tiled=True),
        lax.psum_scatter(proj_b_grad, ("dp", "expert"), scatter_dimension=0, tiled=True),
        lax.psum_scatter(gain_two_grad, ("dp", "expert"), scatter_dimension=0, tiled=True),
        lax.psum_scatter(shift_two_grad, ("dp", "expert"), scatter_dimension=0, tiled=True),
        lax.psum_scatter(router_grad, ("dp", "expert"), scatter_dimension=0, tiled=True),
    )
    return (
        block_out,
        tokens_grad,
        gain_one_sum,
        shift_one_sum,
        qkv_sum,
        query_sum,
        value_sum,
        proj_sum,
        proj_add_sum,
        gain_two_sum,
        shift_two_sum,
        router_sum,
        hidden_w_sum,
        hidden_b_sum,
        return_w_sum,
        return_b_sum,
    )


def solution(mesh):
    in_specs = (
        P(("dp", "expert"), None, None),
        P(("dp", "expert")),
        P(("dp", "expert"), None, None),
        P(("dp", "expert"), None),
        P(("dp", "expert"), None, None),
        P(("dp", "expert")),
        P(("dp", "expert")),
        P(("dp", "expert"), None),
        P(("dp", "expert")),
        P(("dp", "expert")),
        P(("dp", "expert"), None),
        P(("dp", "expert")),
        P(("dp", "expert")),
        P(("dp", "expert")),
        P(("dp", "expert"), None),
        P("expert", "dp", None),
        P("expert", "dp"),
        P("expert", "dp", None),
        P("expert", "dp"),
    )
    out_specs = (
        P(("dp", "expert"), None, None),
        P(("dp", "expert"), None, None),
        P(("dp", "expert")),
        P(("dp", "expert")),
        P(("dp", "expert"), None),
        P(("dp", "expert")),
        P(("dp", "expert")),
        P(("dp", "expert"), None),
        P(("dp", "expert")),
        P(("dp", "expert")),
        P(("dp", "expert")),
        P(("dp", "expert"), None),
        P("expert", "dp", None),
        P("expert", "dp"),
        P("expert", "dp", None),
        P("expert", "dp"),
    )
    return jax.shard_map(
        on_device, mesh=mesh, in_specs=in_specs, out_specs=out_specs, check_vma=False
    )
```

profile of v0, /device:TPU:0, one launch (start us, length us, event | category | flops | bytes accessed | tf_op | source)
XLA Modules:
  0.0 780.9 jit_solution(8550829854829100254)
XLA Ops:
  15.2 42.0 %all-reduce.17 = (bf16[512]{0:T(512)(128)(2,1)S(1)}, bf16[512]{0:T(512)(128)(2,1)S(1)}, bf16[512]{0:T(512)(128)(2,1)S(1)}, bf16[512]{0:T(512)(128)(2,1)S(1)}, bf...) all-reduce(bf16[512]{0:T(512)(128)(2,1)S(1)} %dynamic-update-slice., ...), channel_id=1, replica_groups=mesh['dp'=4,'expert'=8] {'dp','expert'}, use_global_device_ids=true, to_apply=%add.3 | all-reduce | flops 3584 | bytes 14336
  58.0 45.9 %all_gather.54 = bf16[512,512]{1,0:T(8,128)(2,1)} all-gather(bf16[16,512]{1,0:T(8,128)(2,1)S(1)} %copy-done.54), channel_id=1, replica_groups=mesh['dp'=4,'expert'=8] {'dp','expert'}, dimensions={0}, use_global_device_ids=true | all-gather | bytes 540672 | tf_op jit(solution)/shard_map/all_gather | solution.py:128
  103.8 37.4 %all-gather = bf16[32,16,8]{1,2,0:T(8,128)(2,1)S(1)} all-gather(bf16[1,16,8]{1,2,0:T(8,128)(2,1)S(1)} %bitcast.230), channel_id=1, replica_groups=mesh['dp'=4,'expert'=8] {'dp','expert'}, dimensions={0}, use_global_device_ids=true | all-gather | bytes 8448 | tf_op jit(solution)/shard_map/all_gather | solution.py:132
  142.1 7.3 scatter_custom_fusion
  156.5 6.4 scatter_custom_fusion.1
  163.0 11.9 %all_gather.60 = bf16[1,2048]{1,0:T(2,128)(2,1)S(1)} all-gather(bf16[1,512]{1,0:T(2,128)(2,1)S(1)} %copy-done.60), channel_id=1, replica_groups=mesh['dp'=4,'expert'=8] {'dp'}, dimensions={1}, use_global_device_ids=true | all-gather | bytes 5120 | tf_op jit(solution)/shard_map/all_gather | solution.py:191
  174.9 7.7 all_gather.62
  184.9 4.4 gather_fusion.3
  212.9 4.7 gather_fusion.1
  217.6 4.5 all-to-all-start
  225.4 6.4 scatter_custom_fusion.2
  235.5 4.1 all-to-all-done
  243.2 8.6 %fusion.39 = f32[8,152,2048]{2,1,0:T(8,128)} fusion(bf16[8,152,512]{2,1,0:T(8,128)(2,1)} %all-to-all-done, bf16[1,2048,512]{2,1,0:T(8,128)(2,1)} %all-gather.7.cloned.1.call-done), kind=kOutput, calls=%fused_computation.57 | convolution fusion | flops 2550136832 | bytes 13303808 | tf_op jit(solution)/shard_map/sjcd,jfd->sjcf/dot_general | solution.py:196
  251.8 9.4 %fusion.54 = bf16[8,152,512]{2,1,0:T(8,128)(2,1)} fusion(bf16[1,2048,512]{2,1,0:T(8,128)(2,1)} %all-gather.9.cloned.1.call-done, f32[512]{0:T(512)S(1)} %bitcast.231, f32[8,152,2048]{2,1,0:T(8,128)} %fusion.39, f32[2048]{0:T(1024)S(1)} %bitcast.227), kind=kOutput, calls=%fused_computation.68 | convolution fusion | flops 2576285696 | bytes 13314048 | tf_op jit(solution)/shard_map/sjcf,jfd->sjcd/dot_general | solution.py:201
  262.2 4.1 all-to-all-start.1
  269.2 13.4 %fusion.105 = (bf16[2048]{0:T(1024)(128)(2,1)S(1)}, bf16[8,1,152,2048]{3,2,0,1:T(8,128)(2,1)}) fusion(f32[2048]{0:T(1024)S(1)} %bitcast.228, f32[8,152,2048]{2,1,0:T(8,128)} %fusion.39, bf16[8,152,512]{2,1,0:T(8,128)(2,1)} %copy-done.11, bf16[1,2048,512]{2,1,0:T(8,128)(2,1)} %all-gather.9.cloned.1.call-done), kind=kOutput, calls=%fused_computation.179 | convolution fusion | flops 2604922880 | bytes 18296832 | tf_op jit(solution)/shard_map/sjcd,jfd->sjcf/dot_general | solution.py:266
  283.9 4.7 gather_fusion.2
  292.4 7.2 multiply_reduce_fusion.2
  306.3 10.5 %fusion.28 = bf16[1,2048,512]{2,1,0:T(8,128)(2,1)} fusion(bf16[8,152,512]{2,1,0:T(8,128)(2,1)} %copy-done.11, f32[8,152,2048]{2,1,0:T(8,128)} %fusion.39, f32[2048]{0:T(1024)} %bitcast.229), kind=kOutput, calls=%fused_computation.44 | convolution fusion | flops 2576089088 | bytes 13312000 | tf_op jit(solution)/shard_map/sjcf,sjcd->jfd/dot_general | solution.py:279
  316.9 7.1 fusion.25
  324.0 6.9 fusion.41
  331.0 4.3 all-to-all-start.3
  335.8 17.4 %all-to-all-done.3 = bf16[8,152,512]{2,1,0:T(8,128)(2,1)S(1)} async-done(((bf16[8,152,512]{2,1,0:T(8,128)(2,1)}), bf16[8,152,512]{2,1,0:T(8,128)(2,1)S(1)}, u32[]{:S(2)}, u32[]{:S(2)}) %all-to-all-start.3) | async-done | bytes 1245216 | tf_op jit(solution)/shard_map/all_to_all | solution.py:276
  353.1 4.7 gather_fusion.4
  361.5 4.8 multiply_reduce_fusion.1
  375.7 5.9 multiply_reduce_fusion
  387.6 5.2 multiply_convert_fusion.1
  416.2 39.9 %all-reduce.16 = (f32[512]{0:T(512)S(1)}, f32[512]{0:T(512)S(1)}, f32[512]{0:T(512)S(1)}, f32[512]{0:T(512)S(1)}, f32[512]{0:T(512)S(1)}, /*index=5*/f32[512]{0:T(512)S(1)}, f32[512]{0:T(512)S(1)}) all-reduce(f32[512]{0:T(512)S(1)} %get-tuple-element.20, ...), channel_id=2, replica_groups=mesh['dp'=4,'expert'=8] {'dp','expert'}, use_global_device_ids=true, to_apply=%region_28.29.clone | all-reduce | flops 3584 | bytes 28672
  462.8 24.0 %reduce-scatter.20.cloned.1.call-done = bf16[1,512,512]{2,1,0:T(8,128)(2,1)} async-done(((bf16[1,2048,512]{2,1,0:T(8,128)(2,1)}), bf16[1,512,512]{2,1,0:T(8,128)(2,1)}) %reduce-scatter.20.cloned.1.call-update) | async-done | bytes 524304 | tf_op jit(solution)/shard_map/reduce_scatter | solution.py:294
  489.0 43.5 %reduce-scatter.18.cloned.1.call-done = bf16[1,512,512]{2,1,0:T(8,128)(2,1)} async-done(((bf16[1,2048,512]{2,1,0:T(8,128)(2,1)}), bf16[1,512,512]{2,1,0:T(8,128)(2,1)}) %reduce-scatter.18.cloned.1.call-update) | async-done | bytes 524304 | tf_op jit(solution)/shard_map/reduce_scatter | solution.py:288
  534.6 134.8 %reduce-scatter.16.cloned.1.call-done = f32[16,512]{1,0:T(8,128)} async-done(((f32[512,512]{1,0:T(8,128)}), f32[16,512]{1,0:T(8,128)}) %reduce-scatter.16.cloned.1.call-update) | async-done | bytes 32784 | tf_op jit(solution)/shard_map/reduce_scatter | solution.py:381
  669.4 104.3 %reduce-scatter.14.cloned.1.call-done = f32[16,1536]{1,0:T(8,128)} async-done(((f32[512,1536]{1,0:T(8,128)}), f32[16,1536]{1,0:T(8,128)}) %reduce-scatter.14.cloned.1.call-update) | async-done | bytes 98320 | tf_op jit(solution)/shard_map/reduce_scatter | solution.py:378
  (334 shorter events, 121.6 us)
Async XLA Ops:
  7.3 50.0 %copy-start.1 = (bf16[4,144,512]{2,1,0:T(8,128)(2,1)S(1)}, bf16[4,144,512]{2,1,0:T(8,128)(2,1)}, u32[]{:S(2)}) copy-start(bf16[4,144,512]{2,1,0:T(8,128)(2,1)} %param.19) | copy-start | bytes 1769476
  7.3 50.7 %copy-start.54 = (bf16[16,512]{1,0:T(8,128)(2,1)S(1)}, bf16[16,512]{1,0:T(8,128)(2,1)}, u32[]{:S(2)}) copy-start(bf16[16,512]{1,0:T(8,128)(2,1)} %param.29) | copy-start | bytes 49156
  7.3 96.6 %copy-start.59 = (bf16[16,8]{0,1:T(8,128)(2,1)S(1)}, bf16[16,8]{0,1:T(8,128)(2,1)}, u32[]{:S(2)}) copy-start(bf16[16,8]{0,1:T(8,128)(2,1)} %param.33) | copy-start | bytes 772
  7.3 182.3 %all-gather.5.cloned.1.call-start = ((), (), s32[]{:S(2)}) async-start(), calls=%async_computation.11 | async-start | bytes 1622016 | tf_op jit(solution)/shard_map/all_gather | solution.py:125
  8.0 133.5 %copy-start.58 = (s32[1,576]{1,0:T(1,128)S(1)}, s32[1,576]{1,0:T(1,128)}, u32[]{:S(2)}) copy-start(s32[1,576]{1,0:T(1,128)} %param.22) | copy-start | bytes 6916
  8.0 235.1 %all-gather.7.cloned.1.call-start = ((), (), s32[]{:S(2)}) async-start(), calls=%async_computation.12 | async-start | bytes 2621440 | tf_op jit(solution)/shard_map/all_gather | solution.py:190
  8.8 243.0 %all-gather.9.cloned.1.call-start = ((), (), s32[]{:S(2)}) async-start(), calls=%async_computation.13 | async-start | bytes 2621440 | tf_op jit(solution)/shard_map/all_gather | solution.py:192
  11.9 212.5 %copy-start.52 = (pred[576]{0:T(1024)(128)(4,1)}, pred[576]{0:T(1024)(128)(4,1)S(1)}, u32[]{:S(2)}) copy-start(pred[576]{0:T(1024)(128)(4,1)S(1)} %lt.89) | copy-start | bytes 1732
  57.2 132.1 %copy-start.40 = (f32[512]{0:T(512)}, f32[512]{0:T(512)S(1)}, u32[]{:S(2)}) copy-start(f32[512]{0:T(512)S(1)} %convert_element_type.173) | copy-start | bytes 6148
  57.9 83.4 %copy-start.46 = (f32[4,144]{1,0:T(4,128)}, f32[4,144]{1,0:T(4,128)S(1)}, u32[]{:S(2)}) copy-start(f32[4,144]{1,0:T(4,128)S(1)} %multiply_reduce_fusion.9) | copy-start | bytes 6916
  57.9 131.4 %copy-start.35 = (f32[4,144]{1,0:T(4,128)}, f32[4,144]{1,0:T(4,128)S(1)}, u32[]{:S(2)}) copy-start(f32[4,144]{1,0:T(4,128)S(1)} %fusion.85) | copy-start | bytes 6916
  103.8 108.7 %copy-start.50 = (f32[512]{0:T(512)}, f32[512]{0:T(512)S(1)}, u32[]{:S(2)}) copy-start(f32[512]{0:T(512)S(1)} %convert_element_type.185) | copy-start | bytes 6148
  141.4 80.6 %copy-start.33 = (bf16[512,8]{0,1:T(8,128)(2,1)}, bf16[512,8]{0,1:T(8,128)(2,1)S(1)}, u32[]{:S(2)}) copy-start(bf16[512,8]{0,1:T(8,128)(2,1)S(1)} %reshape.615) | copy-start | bytes 24580
  141.5 82.1 %copy-start.43 = (s32[576,2]{0,1:T(2,128)}, s32[576,2]{0,1:T(2,128)S(1)}, u32[]{:S(2)}) copy-start(s32[576,2]{0,1:T(2,128)S(1)} %eq.42) | copy-start | bytes 13828
  152.9 22.0 %copy-start.61 = (bf16[1,128]{1,0:T(2,128)(2,1)S(1)}, bf16[1,128]{1,0:T(2,128)(2,1)}, u32[]{:S(2)}) copy-start(bf16[1,128]{1,0:T(2,128)(2,1)} %param.37) | copy-start | bytes 772
  155.4 28.1 %copy-start.9 = (bf16[4,144,512]{2,1,0:T(8,128)(2,1)S(1)}, bf16[4,144,512]{2,1,0:T(8,128)(2,1)}, u32[]{:S(2)}) copy-start(bf16[4,144,512]{2,1,0:T(8,128)(2,1)} %param.23) | copy-start | bytes 1769476
  174.9 94.3 %copy-start.57 = (f32[1,2048]{1,0:T(1,128)}, f32[1,2048]{1,0:T(1,128)S(1)}, u32[]{:S(2)}) copy-start(f32[1,2048]{1,0:T(1,128)S(1)} %add.278) | copy-start | bytes 24580
  217.6 22.0 %all-to-all-start = ((bf16[8,152,512]{2,1,0:T(8,128)(2,1)}), bf16[8,152,512]{2,1,0:T(8,128)(2,1)}, u32[]{:S(2)}, u32[]{:S(2)}) async-start(bf16[8,152,512]{2,1,0:T(8,128)(2,1)} %bitcast.220), calls=%async_computation | async-start | bytes 2490368 | tf_op jit(solution)/shard_map/all_to_all | solution.py:186
  222.4 13.1 %copy-start.37 = (f32[576]{0:T(1024)}, f32[576]{0:T(1024)S(1)}, u32[]{:S(2)}) copy-start(f32[576]{0:T(1024)S(1)} %fusion.77) | copy-start | bytes 6916
  224.5 11.0 %copy-start.44 = (pred[576,2]{0,1:T(4,128)(4,1)}, pred[576,2]{0,1:T(4,128)(4,1)S(1)}, u32[]{:S(2)}) copy-start(pred[576,2]{0,1:T(4,128)(4,1)S(1)} %copy.159) | copy-start | bytes 3460
  239.6 21.6 %all-to-all-start.2 = ((bf16[8,152,512]{2,1,0:T(8,128)(2,1)}), bf16[8,152,512]{2,1,0:T(8,128)(2,1)S(1)}, u32[]{:S(2)}, u32[]{:S(2)}) async-start(bf16[8,152,512]{2,1,0:T(8,128)(2,1)} %multiply_convert_fusion.2), calls=%async_computation.2 | async-start | bytes 2490368 | tf_op jit(solution)/shard_map/all_to_all | solution.py:263
  262.2 21.6 %all-to-all-start.1 = ((bf16[8,152,512]{2,1,0:T(8,128)(2,1)}), bf16[8,152,512]{2,1,0:T(8,128)(2,1)S(1)}, u32[]{:S(2)}, u32[]{:S(2)}) async-start(bf16[8,152,512]{2,1,0:T(8,128)(2,1)} %fusion.54), calls=%async_computation.1 | async-start | bytes 2490368 | tf_op jit(solution)/shard_map/all_to_all | solution.py:204
  266.3 142.4 %reduce-scatter.26.cloned.1.call-start = ((), (), s32[]{:S(2)}) async-start(), calls=%async_computation.20 | async-start | bytes 163840
  268.7 141.5 %reduce-scatter.24.cloned.1.call-start = ((), (), s32[]{:S(2)}) async-start(), calls=%async_computation.19 | async-start | bytes 655360
  283.8 177.7 %reduce-scatter.22.cloned.1.call-start = ((), (), s32[]{:S(2)}) async-start(), calls=%async_computation.18 | async-start | bytes 270336
  292.4 11.9 %copy-start.5 = (bf16[576,512]{1,0:T(8,128)(2,1)S(1)}, bf16[576,512]{1,0:T(8,128)(2,1)}, u32[]{:S(2)}) copy-start(bf16[576,512]{1,0:T(8,128)(2,1)} %copy-done.4) | copy-start | bytes 1769476
  306.1 180.7 %reduce-scatter.20.cloned.1.call-start = ((), (), s32[]{:S(2)}) async-start(), calls=%async_computation.17 | async-start | bytes 2621440 | tf_op jit(solution)/shard_map/reduce_scatter | solution.py:294
  316.9 215.5 %reduce-scatter.18.cloned.1.call-start = ((), (), s32[]{:S(2)}) async-start(), calls=%async_computation.16 | async-start | bytes 2621440 | tf_op jit(solution)/shard_map/reduce_scatter | solution.py:288
  331.0 22.1 %all-to-all-start.3 = ((bf16[8,152,512]{2,1,0:T(8,128)(2,1)}), bf16[8,152,512]{2,1,0:T(8,128)(2,1)S(1)}, u32[]{:S(2)}, u32[]{:S(2)}) async-start(bf16[8,152,512]{2,1,0:T(8,128)(2,1)} %fusion.41), calls=%async_computation.3 | async-start | bytes 2490368 | tf_op jit(solution)/shard_map/all_to_all | solution.py:276
  335.3 334.1 %reduce-scatter.16.cloned.1.call-start = ((), (), s32[]{:S(2)}) async-start(), calls=%async_computation.15 | async-start | bytes 1081344 | tf_op jit(solution)/shard_map/reduce_scatter | solution.py:381
  381.7 392.0 %reduce-scatter.14.cloned.1.call-start = ((), (), s32[]{:S(2)}) async-start(), calls=%async_computation.14 | async-start | bytes 3244032 | tf_op jit(solution)/shard_map/reduce_scatter | solution.py:378
  415.0 45.3 %copy-start.3 = (f32[576,512]{1,0:T(8,128)S(1)}, f32[576,512]{1,0:T(8,128)}, u32[]{:S(2)}) copy-start(f32[576,512]{1,0:T(8,128)} %copy-done.2) | copy-start | bytes 3538948
  (51 other events, 198.4 us)
Sparse Core Ops, SparseCore 0:
  11.0 57.7 all-gather.4
  70.3 45.7 all-gather.6
  117.7 44.9 all-gather.8
  269.1 19.2 reduce-scatter.25
  290.7 19.8 reduce-scatter.23
  312.7 131.8 reduce-scatter.21
  446.9 39.8 reduce-scatter.19
  489.2 43.1 reduce-scatter.17
  535.3 134.0 reduce-scatter.15
  676.1 97.4 reduce-scatter.13
where the time goes:
time: 791 us; the launch traced here: 781 us
  waiting for transfers between devices  330 us (42%)
  blocking collectives  185 us (23%)
  local copies, waits for them, and re-layouts  93 us (12%)
  matrix products  85.1 us (11%)
  other arithmetic  54.3 us (7%)
  starting transfers between devices  17.6 us (2%)
  between operations  15.9 us (2%)
    reduce_scatter x1, waiting for transfers between devices, on_device(): lax.psum_scatter(proj_w_grad, ('dp', 'expert'), scatter_dimension=0, tile...  135 us
    reduce_scatter x1, waiting for transfers between devices, on_device(): lax.psum_scatter(qkv_w_grad, ('dp', 'expert'), scatter_dimension=0, tiled...  104 us
    unnamed x2, blocking collectives  82 us
    all_gather x1, blocking collectives, on_device(): lax.all_gather(proj_weight, ('dp', 'expert'), axis=0, tiled=True)  45.9 us
    reduce_scatter x1, waiting for transfers between devices, on_device(): lax.psum_scatter(hidden_w_grad.astype(jnp.bfloat16), 'dp', scatter_dimens...  43.5 us
    all_gather x1, blocking collectives, on_device(): lax.all_gather(router_weight, ('dp', 'expert'), axis=0, tiled=True)  37.4 us
    reduce_scatter x1, waiting for transfers between devices, on_device(): lax.psum_scatter(return_w_grad.astype(jnp.bfloat16), 'dp', scatter_dimens...  24 us
    unnamed x169, local copies, waits for them, and re-layouts  18.7 us
  transfers between devices with their start and end apart: 14, of which 6 were waited for; matrix products, arithmetic and copies ran while one was open for 29% of the time, Pallas kernels for 0%

commit v1 on v0

v1 whole, which is shorter than its diff:
```python
import functools
import math

import jax
import jax.numpy as jnp
import numpy as np
from jax import lax
from jax.experimental import pallas as pl
from jax.experimental.pallas import tpu as pltpu
from jax.sharding import PartitionSpec as P

HEADS = 8
QUAD = 4
norm_eps = 1e-06
neg_large = -1e30
F32 = jnp.float32
BF16 = jnp.bfloat16
ROUTER_COL = 32
MISC = 128
GELU_C = math.sqrt(2.0 / math.pi)
GELU_A = 0.044715

NN = (((1,), (0,)), ((), ()))
NT = (((1,), (1,)), ((), ()))
TN = (((0,), (0,)), ((), ()))


def mm(a, b, dims=NN):
    return lax.dot_general(a, b, dims, preferred_element_type=F32)


def params(mib=56):
    return pltpu.CompilerParams(vmem_limit_bytes=mib * 1024 * 1024)


def vmem():
    return pl.BlockSpec(memory_space=pltpu.VMEM)


def smem():
    return pl.BlockSpec(memory_space=pltpu.SMEM)


def normed(values):
    center = values - jnp.mean(values, axis=-1, keepdims=True)
    rstd = lax.rsqrt(jnp.mean(center * center, axis=-1, keepdims=True) + norm_eps)
    return center * rstd, rstd


def norm_back(grad, gain, unit, rstd):
    q = grad * gain
    return rstd * (
        q
        - jnp.mean(q, axis=-1, keepdims=True)
        - unit * jnp.mean(q * unit, axis=-1, keepdims=True)
    )


def masked_softmax(logits, experts):
    lane = lax.broadcasted_iota(jnp.int32, logits.shape, 1)
    inside = (lane >= ROUTER_COL) & (lane < ROUTER_COL + experts)
    logits = jnp.where(inside, logits, neg_large)
    raised = jnp.exp(logits - jnp.max(logits, axis=-1, keepdims=True))
    return raised / jnp.sum(raised, axis=-1, keepdims=True)


def head_stack(rows, head_size):
    lane = lax.broadcasted_iota(jnp.int32, rows.shape, 1) // head_size
    return jnp.concatenate(
        [jnp.where(lane == h, rows, jnp.zeros_like(rows)) for h in range(QUAD)], axis=0
    )


def head_merge(stacked, patches, head_size):
    lane = lax.broadcasted_iota(jnp.int32, (patches, stacked.shape[1]), 1) // head_size
    total = jnp.zeros((patches, stacked.shape[1]), F32)
    for h in range(QUAD):
        total = jnp.where(lane == h, stacked[h * patches : (h + 1) * patches], total)
    return total


def front_kernel(
    dims, scal_ref, cnt_ref, tok_ref, ga_ref, gb_ref, posrow_ref,
    wa_ref, wb_ref, qkv_ref, probs_ref, ctx_ref, hid_ref, rprob_ref, disp_ref,
):
    images, patches, experts, blocks, rels = dims
    width = tok_ref.shape[1]
    head_size = width // HEADS
    rows = ga_ref.shape[1]
    for slot in range(blocks):
        for ref, out, rel in ((ga_ref, wa_ref, rels[0]), (gb_ref, wb_ref, rels[1])):
            at = pl.multiple_of((scal_ref[0] ^ rel[slot]) * rows, rows)
            out[pl.ds(at, rows), :] = ref[slot]
    misc = wb_ref[:, 2 * width :].astype(F32).T
    x = tok_ref[...].astype(F32)
    unit, _ = normed(x)
    first_low = (unit * misc[0:1] + misc[1:2]).astype(BF16)
    qk = mm(first_low, wa_ref[...])
    qkv_ref[:, :width] = (qk[:, :width] + misc[2:3]).astype(BF16)
    qkv_ref[:, width : 2 * width] = qk[:, width:].astype(BF16)
    qkv_ref[:, 2 * width :] = (mm(first_low, wb_ref[:, :width]) + misc[3:4]).astype(BF16)
    scale = 1.0 / math.sqrt(head_size)
    quad_width = QUAD * head_size
    for i in range(images):
        at = slice(i * patches, (i + 1) * patches)
        valid = lax.broadcasted_iota(jnp.int32, (QUAD * patches, patches), 1) < cnt_ref[i]
        for quad in range(HEADS // QUAD):
            lo = quad * quad_width
            q = qkv_ref[at, lo : lo + quad_width]
            k = qkv_ref[at, width + lo : width + lo + quad_width]
            v = qkv_ref[at, 2 * width + lo : 2 * width + lo + quad_width]
            scores = jnp.where(valid, mm(head_stack(q, head_size), k, NT) * scale, neg_large)
            raised = jnp.exp(scores - jnp.max(scores, axis=-1, keepdims=True))
            probs = (raised / jnp.sum(raised, axis=-1, keepdims=True)).astype(BF16)
            probs_ref[i * (HEADS // QUAD) + quad] = probs
            ctx = head_merge(mm(probs, v), patches, head_size)
            ctx_ref[at, lo : lo + quad_width] = ctx.astype(BF16)
    hidden = x + mm(ctx_ref[...], wb_ref[:, width : 2 * width]) + misc[4:5]
    hid_ref[...] = hidden
    unit2, _ = normed(hidden)
    second_low = (unit2 * misc[5:6] + misc[6:7]).astype(BF16)
    rprob_ref[...] = masked_softmax(mm(second_low, wb_ref[:, 2 * width :]), experts)
    slots = disp_ref.shape[0]
    row = lax.broadcasted_iota(jnp.int32, (slots, tok_ref.shape[0]), 0)
    pick = (row == posrow_ref[0:1]) | (row == posrow_ref[1:2])
    disp_ref[...] = mm(pick.astype(F32).astype(BF16), second_low).astype(BF16)


def expert_kernel(
    dims, scal_ref, x_ref, up_ref, w_ref, misc_ref, rb_ref,
    out_ref, ing_ref, dw_ref, g_scr, acc_o, acc_i, dwh, dwr, drb,
):
    experts, tile, parts = dims
    slots, width = x_ref.shape
    share = (w_ref.shape[1] - 16) // 2
    c = pl.program_id(0)

    @pl.when(c == 0)
    def _():
        prob = masked_softmax(mm(x_ref[...], misc_ref[...]), experts)
        lane = lax.broadcasted_iota(jnp.int32, prob.shape, 1)
        mine = lane == ROUTER_COL + scal_ref[1]
        gate = jnp.sum(jnp.where(mine, prob, 0.0), axis=-1, keepdims=True)
        low = (gate * up_ref[...].astype(F32)).astype(BF16)
        g_scr[...] = low
        drb[...] = jnp.sum(low.astype(F32), axis=0, keepdims=True)
        acc_o[...] = jnp.broadcast_to(rb_ref[...], acc_o.shape)
        acc_i[...] = jnp.zeros_like(acc_i)

    wh = w_ref[0, :share]
    wr = w_ref[0, share : 2 * share]
    hb = w_ref[0, 2 * share : 2 * share + 16].astype(F32)[0:1, :share]
    dwh[...] = jnp.zeros_like(dwh)
    dwr[...] = jnp.zeros_like(dwr)

    def body(t, dhb):
        at = pl.ds(pl.multiple_of(t * tile, 16), tile)
        x = x_ref[at, :]
        g = g_scr[at, :]
        pre = mm(x, wh, NT) + hb
        square = pre * pre
        tanh = jnp.tanh(GELU_C * pre * (1.0 + GELU_A * square))
        half = 0.5 * (1.0 + tanh)
        act = (pre * half).astype(BF16)
        slope = half + (0.5 * GELU_C) * pre * (1.0 - tanh * tanh) * (1.0 + 3.0 * GELU_A * square)
        pg = (mm(g, wr, NT) * slope).astype(BF16)
        acc_o[at, :] += mm(act, wr)
        acc_i[at, :] += mm(pg, wh)
        dwr[...] += mm(act, g, TN)
        dwh[...] += mm(pg, x, TN)
        return dhb + jnp.sum(pg.astype(F32), axis=0, keepdims=True)

    dhb = lax.fori_loop(0, slots // tile, body, jnp.zeros((1, share), F32))
    dw_ref[0, :share] = dwh[...].astype(BF16)
    dw_ref[0, share : 2 * share] = dwr[...].astype(BF16)
    if share < width:
        dhb = jnp.concatenate([dhb, jnp.zeros((1, width - share), F32)], axis=1)
    row = lax.broadcasted_iota(jnp.int32, (16, width), 0)
    piece = width // parts
    for j in range(parts):

        @pl.when(c == j)
        def _():
            own = jnp.concatenate(
                [drb[:, j * piece : (j + 1) * piece], jnp.zeros((1, width - piece), F32)], axis=1
            )
            tail = jnp.where(row == 0, dhb, jnp.where(row == 1, own, 0.0))
            dw_ref[0, 2 * share :] = tail.astype(BF16)

    @pl.when(c == pl.num_programs(0) - 1)
    def _():
        out_ref[...] = acc_o[...].astype(BF16)
        ing_ref[...] = acc_i[...].astype(BF16)


def back_kernel(
    dims, scal_ref, tok_ref, up_ref, ret_ref, ing_ref, hid_ref, rprob_ref, poscol_ref,
    wa_ref, wb_ref, qkv_ref, probs_ref, ctx_ref,
    block_ref, tgrad_ref, ga_ref, gb_ref, dqkv_ref, cg_ref,
):
    images, patches, experts, blocks, slots_of = dims
    tokens, width = tok_ref.shape
    head_size = width // HEADS
    slots = ret_ref.shape[0]
    rows = ga_ref.shape[1]
    misc = wb_ref[:, 2 * width :].astype(F32).T
    hidden = hid_ref[...]
    up = up_ref[...].astype(F32)
    rprob = rprob_ref[...]
    lane = lax.broadcasted_iota(jnp.int32, (tokens, slots), 1)
    rlane = lax.broadcasted_iota(jnp.int32, (tokens, MISC), 1)
    pos = [poscol_ref[:, k : k + 1] for k in range(2)]
    mixed = hidden
    prob_grad = jnp.zeros((tokens, MISC), F32)
    for k in range(2):
        picked = mm((lane == pos[k]).astype(F32).astype(BF16), ret_ref[...])
        hot = (rlane == ROUTER_COL + poscol_ref[:, 2 + k : 3 + k]) & (pos[k] >= 0)
        gate = jnp.sum(jnp.where(hot, rprob, 0.0), axis=-1, keepdims=True)
        mixed = mixed + gate * picked
        gate_grad = jnp.sum(up * picked, axis=-1, keepdims=True)
        prob_grad = prob_grad + jnp.where(hot, gate_grad, 0.0)
    block_ref[...] = mixed.astype(BF16)
    logit_low = (
        rprob * (prob_grad - jnp.sum(prob_grad * rprob, axis=-1, keepdims=True))
    ).astype(BF16)
    unit2, rstd2 = normed(hidden)
    second_low = (unit2 * misc[5:6] + misc[6:7]).astype(BF16)
    router_grad = mm(second_low, logit_low, TN)
    either = ((lane == pos[0]) | (lane == pos[1])).astype(F32).astype(BF16)
    second_grad = mm(logit_low, wb_ref[:, 2 * width :], NT) + mm(either, ing_ref[...])
    gain2_grad = jnp.sum(second_grad * unit2, axis=0, keepdims=True)
    shift2_grad = jnp.sum(second_grad, axis=0, keepdims=True)
    residual = up + norm_back(second_grad, misc[5:6], unit2, rstd2)
    proj_in = residual.astype(BF16)
    proj_b_grad = jnp.sum(proj_in.astype(F32), axis=0, keepdims=True)
    proj_w_grad = mm(ctx_ref[...], proj_in, TN)
    cg_ref[...] = mm(proj_in, wb_ref[:, width : 2 * width], NT).astype(BF16)
    scale = 1.0 / math.sqrt(head_size)
    quad_width = QUAD * head_size
    for i in range(images):
        at = slice(i * patches, (i + 1) * patches)
        for quad in range(HEADS // QUAD):
            lo = quad * quad_width
            q = qkv_ref[at, lo : lo + quad_width]
            k = qkv_ref[at, width + lo : width + lo + quad_width]
            v = qkv_ref[at, 2 * width + lo : 2 * width + lo + quad_width]
            cg = head_stack(cg_ref[at, lo : lo + quad_width], head_size)
            probs_low = probs_ref[i * (HEADS // QUAD) + quad]
            probs = probs_low.astype(F32)
            weight_grad = mm(cg, v, NT)
            value_grad = mm(probs_low, cg, TN)
            score_grad = (
                probs * (weight_grad - jnp.sum(weight_grad * probs, axis=-1, keepdims=True))
            ).astype(BF16)
            query_grad = head_merge(mm(score_grad, k), patches, head_size) * scale
            key_grad = mm(score_grad, head_stack(q, head_size), TN) * scale
            dqkv_ref[at, lo : lo + quad_width] = query_grad.astype(BF16)
            dqkv_ref[at, width + lo : width + lo + quad_width] = key_grad.astype(BF16)
            dqkv_ref[at, 2 * width + lo : 2 * width + lo + quad_width] = value_grad.astype(BF16)
    unit1, rstd1 = normed(tok_ref[...].astype(F32))
    first_low = (unit1 * misc[0:1] + misc[1:2]).astype(BF16)
    query_b_grad = jnp.sum(dqkv_ref[:, :width].astype(F32), axis=0, keepdims=True)
    value_b_grad = jnp.sum(dqkv_ref[:, 2 * width :].astype(F32), axis=0, keepdims=True)
    first_grad = mm(dqkv_ref[:, : 2 * width], wa_ref[...], NT) + mm(
        dqkv_ref[:, 2 * width :], wb_ref[:, :width], NT
    )
    gain1_grad = jnp.sum(first_grad * unit1, axis=0, keepdims=True)
    shift1_grad = jnp.sum(first_grad, axis=0, keepdims=True)
    tgrad_ref[...] = (residual + norm_back(first_grad, misc[0:1], unit1, rstd1)).astype(BF16)
    small = jnp.concatenate(
        [
            gain1_grad, shift1_grad, query_b_grad, value_b_grad,
            proj_b_grad, gain2_grad, shift2_grad, jnp.zeros((MISC - 7, width), F32),
        ],
        axis=0,
    )
    tail = (router_grad + small.T).astype(BF16)
    first_t = first_low.astype(F32).T.astype(BF16)
    da = mm(first_t, dqkv_ref[:, : 2 * width]).astype(BF16)
    dv = mm(first_t, dqkv_ref[:, 2 * width :]).astype(BF16)
    db = jnp.concatenate([dv, proj_w_grad.astype(BF16), tail], axis=1)
    for r in range(blocks):
        ga_ref[slots_of[0][r] ^ scal_ref[2]] = da[r * rows : (r + 1) * rows]
        gb_ref[slots_of[1][r] ^ scal_ref[3]] = db[r * rows : (r + 1) * rows]


def flip(x, stage):
    axis, size, bit = stage
    return lax.ppermute(x, axis, [(i, i ^ bit) for i in range(size)])


def bits_of(size):
    return [1 << b for b in range(size.bit_length() - 1)]


def plan(dp, ex):
    dp_stages = [("dp", dp, b) for b in reversed(bits_of(dp))]
    chip = [("expert", ex, b) for b in bits_of(ex)[1:]]
    half = len(chip) // 2
    core = ("expert", ex, 1)
    return dp_stages, chip, chip[half:] + chip[:half], core


def code_of(stage, ex):
    axis, _, bit = stage
    return bit * ex if axis == "dp" else bit


def slot_codes(stages, ex):
    rel = [0]
    for stage in stages:
        rel = rel + [r ^ code_of(stage, ex) for r in rel]
    return rel


def on_device(
    tokens, patch_counts, expert_ids, priority, out_grad, first_gain, first_shift, qkv_weight,
    query_bias, value_bias, proj_weight, proj_bias, second_gain, second_shift, router_weight,
    hidden_weight, hidden_bias, return_weight, return_bias, *, dp, ex,
):
    images, patches, width = tokens.shape
    count = images * patches
    top = expert_ids.shape[2]
    experts = router_weight.shape[1]
    capacity = (count * top * 105 + 100 * experts - 1) // (100 * experts)
    slots = experts * capacity
    devices = dp * ex
    share_rows = qkv_weight.shape[0]
    ff_share = hidden_weight.shape[1]
    dp_at = lax.axis_index("dp")
    ex_at = lax.axis_index("expert")
    me = dp_at * ex + ex_at

    tail = jnp.zeros((16, width), BF16)
    tail = tail.at[0, :ff_share].set(hidden_bias[0]).at[1, : width // dp].set(return_bias[0])
    pack = jnp.concatenate([hidden_weight[0], return_weight[0], tail], axis=0)
    expert_w = lax.all_gather(pack, "dp", axis=0)
    return_add = expert_w[:, 2 * ff_share + 1, : width // dp].reshape(1, width).astype(F32)

    dp_stages, chip_a, chip_b, core = plan(dp, ex)
    small = jnp.stack(
        [first_gain, first_shift, query_bias, value_bias, proj_bias, second_gain, second_shift],
        axis=1,
    )
    small = jnp.concatenate(
        [
            small,
            jnp.zeros((share_rows, ROUTER_COL - 7), BF16),
            router_weight,
            jnp.zeros((share_rows, MISC - ROUTER_COL - experts), BF16),
        ],
        axis=1,
    )
    packed = jnp.concatenate([qkv_weight, proj_weight, small], axis=1)[None]
    for stage in dp_stages:
        packed = jnp.concatenate([packed, flip(packed, stage)], axis=0)
    parts = [packed[..., : 2 * width], packed[..., 2 * width :]]
    for stages in zip(chip_a, chip_b):
        parts = [jnp.concatenate([p, flip(p, s)], axis=0) for p, s in zip(parts, stages)]
    parts = [jnp.concatenate([p, flip(p, core)], axis=0) for p in parts]
    orders = [dp_stages + list(c) + [core] for c in (chip_a, chip_b)]
    rels = [slot_codes(o, ex) for o in orders]
    in_kernel = share_rows % 16 == 0
    if in_kernel:
        blocks, block_rows, gather_at = devices, share_rows, me
        kernel_rels = rels
    else:
        blocks, block_rows, gather_at = width // 16, 16, jnp.int32(0)
        kernel_rels = [list(range(blocks))] * 2
        back = [np.argsort(np.array(r)) for r in rels]
        parts = [
            p[jnp.asarray(b)[jnp.arange(devices) ^ me]].reshape(blocks, 16, -1)
            for p, b in zip(parts, back)
        ]

    valid = (
        lax.broadcasted_iota(jnp.int32, (images, patches), 1) < patch_counts[:, None]
    ).reshape(count)
    choices = expert_ids.reshape(count, top)
    rank = priority[0]
    earlier = (rank[:, None] > rank[None, :]).astype(BF16)
    iota = jnp.arange(experts, dtype=jnp.int32)
    hot = choices[:, :, None] == iota[None, None, :]
    hot_valid = (hot & valid[:, None, None]).astype(BF16).reshape(count, top * experts)
    before = jnp.dot(earlier, hot_valid, preferred_element_type=F32).reshape(count, top, experts)
    totals = jnp.sum(hot_valid.astype(F32), axis=0).reshape(top, experts)
    start = jnp.cumsum(totals, axis=0) - totals
    slot = jnp.sum(jnp.where(hot, before + start[None], 0.0), axis=-1).astype(jnp.int32)
    kept = valid[:, None] & (slot < capacity)
    pos = jnp.where(kept, choices * capacity + slot, -1)
    pos_row = pos.T
    pos_col = jnp.concatenate([pos, choices], axis=1)

    pick = jnp.zeros((slots, count), jnp.bool_)
    slot_iota = lax.broadcasted_iota(jnp.int32, (slots, count), 0)
    for k in range(top):
        pick = pick | (slot_iota == pos_row[k][None, :])
    up = out_grad.reshape(count, width)
    up_slots = jnp.dot(pick.astype(BF16), up, preferred_element_type=F32).astype(BF16)

    def exchange(x):
        x = lax.all_to_all(
            x.reshape(experts, capacity, width), "expert", split_axis=0, concat_axis=0, tiled=True
        )
        return x.reshape(slots, width)

    up_arrived = exchange(up_slots)

    tables = [np.argsort(np.array(r)) for r in rels]
    if in_kernel:
        send_at = [jnp.asarray(t, jnp.int32)[me] for t in tables]
        kernel_slots = [[int(v) for v in t] for t in tables]
    else:
        send_at = [jnp.int32(0), jnp.int32(0)]
        kernel_slots = [list(range(blocks))] * 2
    scal = jnp.stack([gather_at, ex_at, send_at[0], send_at[1]]).astype(jnp.int32)

    tok = tokens.reshape(count, width)
    pairs = images * (HEADS // QUAD)
    wa, wb, qkv, probs, ctx, hidden, rprob, dispatch = pl.pallas_call(
        functools.partial(front_kernel, (images, patches, experts, blocks, kernel_rels)),
        out_shape=(
            jax.ShapeDtypeStruct((width, 2 * width), BF16),
            jax.ShapeDtypeStruct((width, 2 * width + MISC), BF16),
            jax.ShapeDtypeStruct((count, 3 * width), BF16),
            jax.ShapeDtypeStruct((pairs, QUAD * patches, patches), BF16),
            jax.ShapeDtypeStruct((count, width), BF16),
            jax.ShapeDtypeStruct((count, width), F32),
            jax.ShapeDtypeStruct((count, MISC), F32),
            jax.ShapeDtypeStruct((slots, width), BF16),
        ),
        in_specs=[smem(), smem()] + [vmem()] * 4,
        out_specs=(vmem(),) * 8,
        compiler_params=params(),
        name="front",
    )(scal, patch_counts, tok, parts[0], parts[1], pos_row)

    arrived = exchange(dispatch)

    tile = 304 if slots % 304 == 0 else slots
    whole = lambda shape: pl.BlockSpec(shape, lambda c: (0,) * len(shape))
    pack_rows = pack.shape[0]
    expert_out, in_grad, dw = pl.pallas_call(
        functools.partial(expert_kernel, (experts, tile, dp)),
        grid=(dp,),
        out_shape=(
            jax.ShapeDtypeStruct((slots, width), BF16),
            jax.ShapeDtypeStruct((slots, width), BF16),
            jax.ShapeDtypeStruct((dp, pack_rows, width), BF16),
        ),
        in_specs=[
            smem(),
            whole((slots, width)),
            whole((slots, width)),
            pl.BlockSpec((1, pack_rows, width), lambda c: (c, 0, 0)),
            whole((width, MISC)),
            whole((1, width)),
        ],
        out_specs=(
            whole((slots, width)),
            whole((slots, width)),
            pl.BlockSpec((1, pack_rows, width), lambda c: (c, 0, 0)),
        ),
        scratch_shapes=[
            pltpu.VMEM((slots, width), BF16),
            pltpu.VMEM((slots, width), F32),
            pltpu.VMEM((slots, width), F32),
            pltpu.VMEM((ff_share, width), F32),
            pltpu.VMEM((ff_share, width), F32),
            pltpu.VMEM((1, width), F32),
        ],
        compiler_params=params(),
        name="experts",
    )(scal, arrived, up_arrived, expert_w, wb[:, 2 * width :], return_add)

    returned = exchange(expert_out)
    grad_back = exchange(in_grad)
    dw_sum = lax.psum_scatter(dw, "dp", scatter_dimension=0, tiled=False).astype(F32)

    block_out, tokens_grad, da, db = pl.pallas_call(
        functools.partial(back_kernel, (images, patches, experts, blocks, kernel_slots)),
        out_shape=(
            jax.ShapeDtypeStruct((count, width), BF16),
            jax.ShapeDtypeStruct((count, width), BF16),
            jax.ShapeDtypeStruct((blocks, block_rows, 2 * width), BF16),
            jax.ShapeDtypeStruct((blocks, block_rows, 2 * width + MISC), BF16),
        ),
        in_specs=[smem()] + [vmem()] * 12,
        out_specs=(vmem(),) * 4,
        scratch_shapes=[pltpu.VMEM((count, 3 * width), BF16), pltpu.VMEM((count, width), BF16)],
        compiler_params=params(),
        name="back",
    )(scal, tok, up, returned, grad_back, hidden, rprob, pos_col, wa, wb, qkv, probs, ctx)

    sums = [da, db]
    if not in_kernel:
        sums = [
            s.reshape(devices, share_rows, -1)[jnp.asarray(np.array(r)) ^ me]
            for s, r in zip(sums, rels)
        ]
    for stages in zip(*[list(reversed(o)) for o in orders]):
        halves = [s.reshape(2, -1, *s.shape[1:]) for s in sums]
        came = [flip(h[1], st) for h, st in zip(halves, stages)]
        sums = [
            (h[0].astype(F32) + c.astype(F32)).astype(BF16) for h, c in zip(halves, came)
        ]
    ga, gb = [s[0].astype(F32) for s in sums]
    qkv_sum = jnp.concatenate([ga, gb[:, :width]], axis=1)
    proj_sum = gb[:, width : 2 * width]
    vec = [gb[:, 2 * width + j] for j in range(7)]
    router_sum = gb[:, 2 * width + ROUTER_COL : 2 * width + ROUTER_COL + experts]
    return (
        block_out.reshape(tokens.shape),
        tokens_grad.reshape(tokens.shape),
        vec[0], vec[1], qkv_sum, vec[2], vec[3], proj_sum, vec[4], vec[5], vec[6], router_sum,
        dw_sum[:ff_share][None],
        dw_sum[2 * ff_share, :ff_share][None],
        dw_sum[ff_share : 2 * ff_share][None],
        dw_sum[2 * ff_share + 1, : width // dp][None],
    )


def solution(mesh):
    both, rows = P(("dp", "expert")), P(("dp", "expert"), None)
    cube = P(("dp", "expert"), None, None)
    weight, bias = P("expert", "dp", None), P("expert", "dp")
    in_specs = (
        cube, both, cube, rows, cube, both, both, rows, both, both, rows, both, both, both, rows,
        weight, bias, weight, bias,
    )
    out_specs = (
        cube, cube, both, both, rows, both, both, rows, both, both, both, rows,
        weight, bias, weight, bias,
    )
    return jax.shard_map(
        functools.partial(on_device, dp=mesh.shape["dp"], ex=mesh.shape["expert"]),
        mesh=mesh,
        in_specs=in_specs,
        out_specs=out_specs,
        check_vma=False,
    )
```

time: 791 us -> 237 us (0.30); the launches traced: 781 us -> 236 us
  waiting for transfers between devices: 330 us -> 78.2 us
  blocking collectives: 185 us -> 21 us
  matrix products: 85.1 us -> 2.68 us
  local copies, waits for them, and re-layouts: 93 us -> 18 us
  Pallas kernels: 0 us -> 58.5 us
  other arithmetic: 54.3 us -> 13.2 us
  starting transfers between devices: 17.6 us -> 29.9 us
    reduce_scatter x4 -> x1, waiting for transfers between devices: 307 us -> 0.01 us  [on_device(): lax.psum_scatter(dw, 'dp', scatter_dimension=0, tiled=False).astype(F32)]
    all_gather x4 -> x0, blocking collectives: 103 us -> none  [the longest x1 45.9 us: on_device(): lax.all_gather(proj_weight, ('dp', 'expert'), axis=0, tiled=True)]
    unnamed x2 -> x0, blocking collectives: 82 us -> none
    dot_general x20 -> x2, matrix products: 83.3 us -> 2.68 us  [the longest x1 2.23 us: on_device(): jnp.dot(pick.astype(BF16), up, preferred_element_type=F32).astype(BF16)]
    pallas_call x0 -> x3, Pallas kernels: none -> 58.5 us  [the longest x1 32.6 us: on_device(): pl.pallas_call(functools.partial(expert_kernel, (experts, tile, dp)), gri...]
    all_gather x3 -> x1, waiting for transfers between devices: 0.04 us -> 30.8 us  [on_device(): expert_w = lax.all_gather(pack, 'dp', axis=0)]
    ppermute x0 -> x18, waiting for transfers between devices: none -> 29.9 us  [flip(): return lax.ppermute(x, axis, [(i, i ^ bit) for i in range(size)])]
    reduce_sum x18 -> x1, other arithmetic: 22.8 us -> 0.1 us  [on_device(): totals = jnp.sum(hot_valid.astype(F32), axis=0).reshape(top, experts)]
  transfers between devices with their start and end apart: 14 -> 23, of which waited for: 6 -> 17; matrix products, arithmetic and copies ran while one was open for 29% -> 9% of each run, Pallas kernels for 0% -> 11%
where the time goes in v1:
time: 237 us; the launch traced here: 236 us
  waiting for transfers between devices  78.2 us (33%)
  Pallas kernels  58.5 us (25%)
  starting transfers between devices  29.9 us (13%)
  blocking collectives  21 us (9%)
  local copies, waits for them, and re-layouts  18 us (8%)
  between operations  14.5 us (6%)
  other arithmetic  13.2 us (6%)
  matrix products  2.68 us (1%)
    pallas_call x1, Pallas kernels, on_device(): pl.pallas_call(functools.partial(expert_kernel, (experts, tile, dp)), gri...  32.6 us
    all_gather x1, waiting for transfers between devices, on_device(): expert_w = lax.all_gather(pack, 'dp', axis=0)  30.8 us
    ppermute x18, waiting for transfers between devices, flip(): return lax.ppermute(x, axis, [(i, i ^ bit) for i in range(size)])  29.9 us
    all_to_all x1, blocking collectives, exchange(): lax.all_to_all(x.reshape(experts, capacity, width), 'expert', split_axis=...  21 us
    ppermute x18, starting transfers between devices, flip(): return lax.ppermute(x, axis, [(i, i ^ bit) for i in range(size)])  18.9 us
    all_to_all x3, waiting for transfers between devices, exchange(): lax.all_to_all(x.reshape(experts, capacity, width), 'expert', split_axis=...  17.4 us
    pallas_call x1, Pallas kernels, on_device(): pl.pallas_call(functools.partial(back_kernel, (images, patches, experts,...  17.2 us
    all_to_all x3, starting transfers between devices, exchange(): lax.all_to_all(x.reshape(experts, capacity, width), 'expert', split_axis=...  10.8 us
  transfers between devices with their start and end apart: 23, of which 17 were waited for; matrix products, arithmetic and copies ran while one was open for 9% of the time, Pallas kernels for 11%

profile of v1, /device:TPU:0, one launch (start us, length us, event | category | flops | bytes accessed | tf_op | source)
XLA Modules:
  0.0 236.1 jit_solution(14115692745183610498)
XLA Ops:
  8.8 2.4 %pad_maximum_fusion.1 = bf16[1040,512]{1,0:T(8,128)(2,1)} fusion(bf16[16,512]{1,0:T(8,128)(2,1)S(1)} %scatter.9, bf16[512,512]{1,0:T(8,128)(2,1)} %bitcast.85, bf16[512,512]{1,0:T(8,128)(2,1)} %bitcast.86), kind=kLoop, calls=%fused_computation.15 | loop fusion | flops 3194880 | bytes 2129920 | tf_op jit(solution)/shard_map/concatenate | solution.py:336
  12.2 4.1 %collective-permute-start = (bf16[1,16,2176]{2,1,0:T(8,128)(2,1)S(1)}, bf16[1,16,2176]{2,1,0:T(8,128)(2,1)S(1)}, u32[]{:S(2)}, u32[]{:S(2)}) collective-permute-start(bf16[1,16,2176]{2,1,0:T(8,128)(2,1)S(1)} %bitcast.79), channel_id=1, source_target_pairs={{0,16},{8,24},{16,0},{24,8},{1,17},{9,25},{17,1},{25,9},{2,18},{10... | collective-permute-start | bytes 208904 | tf_op jit(solution)/shard_map/ppermute | solution.py:289
  17.2 2.8 %collective-permute-done = bf16[1,16,2176]{2,1,0:T(8,128)(2,1)S(1)} collective-permute-done((bf16[1,16,2176]{2,1,0:T(8,128)(2,1)S(1)}, bf16[1,16,2176]{2,1,0:T(8,128)(2,1)S(1)}, u32[]{:S(2)}, u32[]{:S(2)}) %collective-permute-start) | collective-permute-done | bytes 69664 | tf_op jit(solution)/shard_map/ppermute | solution.py:289
  20.8 4.4 %collective-permute-done.1 = bf16[2,16,2176]{2,1,0:T(8,128)(2,1)S(1)} collective-permute-done((bf16[2,16,2176]{2,1,0:T(8,128)(2,1)S(1)}, bf16[2,16,2176]{2,1,0:T(8,128)(2,1)S(1)}, u32[]{:S(2)}, u32[]{:S(2)}) %collective-permute-start.1) | collective-permute-done | bytes 139296 | tf_op jit(solution)/shard_map/ppermute | solution.py:289
  25.2 2.3 collective-permute-start.2
  27.6 1.7 collective-permute-start.5
  30.5 2.4 %collective-permute-start.3 = (bf16[8,16,1024]{2,1,0:T(8,128)(2,1)S(1)}, bf16[8,16,1024]{2,1,0:T(8,128)(2,1)S(1)}, u32[]{:S(2)}, u32[]{:S(2)}) collective-permute-start(bf16[8,16,1024]{2,1,0:T(8,128)(2,1)S(1)} %pad_maximum_fusion.6), channel_id=1, source_target_pairs={{0,4},{1,5},{2,6},{3,7},{4,0},{5,1},{6,2},{7,3},{8,12},{9,13},{10,... | collective-permute-start | bytes 786440 | tf_op jit(solution)/shard_map/ppermute | solution.py:289
  33.9 1.6 collective-permute-start.6
  35.5 2.2 fusion.3
  37.7 3.6 %all-to-all-start.1 = ((bf16[8,152,512]{2,1,0:T(8,128)(2,1)}), bf16[8,152,512]{2,1,0:T(8,128)(2,1)S(1)}, u32[]{:S(2)}, u32[]{:S(2)}) async-start(bf16[8,152,512]{2,1,0:T(8,128)(2,1)} %bitcast.19), calls=%async_computation.1 | async-start | bytes 2490368 | tf_op jit(solution)/shard_map/all_to_all | solution.py:402
  44.0 1.9 pad_add_fusion.1.scal_ref
  45.9 2.1 pad_maximum_fusion.2.ga_ref
  49.2 8.7 %front.1 = (bf16[512,1024]{1,0:T(8,128)(2,1)}, bf16[512,1152]{1,0:T(8,128)(2,1)}, bf16[576,1536]{1,0:T(8,128)(2,1)}, bf16[8,576,144]{2,1,0:T(8,128)(2,1)}, bf16[...) custom-call(s32[4]{0:T(128)} %pad_add_fusion.1.scal_ref, s32[4]{0:T(128)} %cnt_ref.1, ...), custom_call_target="tpu_custom_call" | custom-call | tf_op jit(solution)/shard_map/front/pallas_call | solution.py:420
  59.8 3.6 %all-to-all-start = ((bf16[8,152,512]{2,1,0:T(8,128)(2,1)}), bf16[8,152,512]{2,1,0:T(8,128)(2,1)S(1)}, u32[]{:S(2)}, u32[]{:S(2)}) async-start(bf16[8,152,512]{2,1,0:T(8,128)(2,1)} %bitcast.77), calls=%async_computation | async-start | bytes 2490368 | tf_op jit(solution)/shard_map/all_to_all | solution.py:402
  63.6 1.6 slice.182.misc_ref
  65.2 30.8 %all-gather.3.cloned.1.call-done = bf16[4160,512]{1,0:T(8,128)(2,1)} async-done(((bf16[1040,512]{1,0:T(8,128)(2,1)}), bf16[4160,512]{1,0:T(8,128)(2,1)}) %all-gather.3.cloned.1.call-update) | async-done | bytes 4259856 | tf_op jit(solution)/shard_map/all_gather | solution.py:337
  96.0 1.3 fusion.34.rb_ref
  98.3 32.6 %experts.1 = (bf16[1216,512]{1,0:T(8,128)(2,1)}, bf16[1216,512]{1,0:T(8,128)(2,1)}, bf16[4,1040,512]{2,1,0:T(8,128)(2,1)}) custom-call(s32[4]{0:T(128)} %pad_add_fusion.1.scal_ref, bf16[1216,512]{1,0:T(8,128)(2,1)} %bitcast.70, bf16[1216,512]{1,0:T(8,128)(2,1)} %bitcast.69, bf16[4,1040,512]{2,1,0:T(8,128)(2,1)} %bitcast.74, ...), custom_call_target="tpu_custom_call" | custom-call | tf_op jit(solution)/shard_map/experts/pallas_call | solution.py:443
  130.9 1.3 copy-done.4
  132.2 21.0 %all_to_all.20 = bf16[8,152,512]{2,1,0:T(8,128)(2,1)} all-to-all(bf16[8,152,512]{2,1,0:T(8,128)(2,1)S(1)} %bitcast.78), channel_id=1, replica_groups=mesh['dp'=4,'expert'=8] {'expert'}, dimensions={0} | all-to-all | bytes 2490368 | tf_op jit(solution)/shard_map/all_to_all | solution.py:402
  153.2 3.7 %all-to-all-start.3 = ((bf16[8,152,512]{2,1,0:T(8,128)(2,1)}), bf16[8,152,512]{2,1,0:T(8,128)(2,1)S(1)}, u32[]{:S(2)}, u32[]{:S(2)}) async-start(bf16[8,152,512]{2,1,0:T(8,128)(2,1)} %bitcast.27), calls=%async_computation.3 | async-start | bytes 2490368 | tf_op jit(solution)/shard_map/all_to_all | solution.py:402
  157.8 16.5 %all-to-all-done.3 = bf16[8,152,512]{2,1,0:T(8,128)(2,1)S(1)} async-done(((bf16[8,152,512]{2,1,0:T(8,128)(2,1)}), bf16[8,152,512]{2,1,0:T(8,128)(2,1)S(1)}, u32[]{:S(2)}, u32[]{:S(2)}) %all-to-all-start.3) | async-done | bytes 1245216 | tf_op jit(solution)/shard_map/all_to_all | solution.py:402
  175.4 17.2 %back.1 = (bf16[576,512]{1,0:T(8,128)(2,1)}, bf16[576,512]{1,0:T(8,128)(2,1)}, bf16[32,16,1024]{2,1,0:T(8,128)(2,1)}, bf16[32,16,1152]{2,1,0:T(8,128)(2,1)}) custom-call(s32[4]{0:T(128)} %pad_add_fusion.1.scal_ref, bf16[576,512]{1,0:T(8,128)(2,1)} %bitcast.76, bf16[576,512]{1,0:T(8,128)(2,1)} %bitcast.83, bf16[1216,512]{1,0:T(8,128)(2,1)} %bitcast.71, ...), custom_call_target="tpu_custom_call" | custom-call | tf_op jit(solution)/shard_map/back/pallas_call | solution.py:480
  198.0 6.4 %collective-permute-done.14 = bf16[8,16,1024]{2,1,0:T(8,128)(2,1)S(1)} collective-permute-done((bf16[8,16,1024]{2,1,0:T(8,128)(2,1)S(1)}, bf16[8,16,1024]{2,1,0:T(8,128)(2,1)S(1)}, u32[]{:S(2)}, u32[]{:S(2)}) %collective-permute-start.14) | collective-permute-done | bytes 262176 | tf_op jit(solution)/shard_map/ppermute | solution.py:289
  205.1 1.7 collective-permute-done.9
  207.5 2.0 collective-permute-done.15
  209.7 2.6 %collective-permute-done.10 = bf16[4,16,1152]{2,1,0:T(8,128)(2,1)S(1)} collective-permute-done((bf16[4,16,1152]{2,1,0:T(8,128)(2,1)S(1)}, bf16[4,16,1152]{2,1,0:T(8,128)(2,1)S(1)}, u32[]{:S(2)}, u32[]{:S(2)}) %collective-permute-start.10) | collective-permute-done | bytes 147488 | tf_op jit(solution)/shard_map/ppermute | solution.py:289
  212.4 1.8 collective-permute-done.16
  215.4 1.3 collective-permute-done.11
  219.2 2.6 %collective-permute-done.12 = bf16[1,16,1152]{2,1,0:T(8,128)(2,1)S(1)} collective-permute-done((bf16[1,16,1152]{2,1,0:T(8,128)(2,1)S(1)}, bf16[1,16,1152]{2,1,0:T(8,128)(2,1)S(1)}, u32[]{:S(2)}, u32[]{:S(2)}) %collective-permute-start.12) | collective-permute-done | bytes 36896 | tf_op jit(solution)/shard_map/ppermute | solution.py:289
  224.6 1.9 convert_bitcast_fusion
  227.6 1.6 fusion.35
  (143 shorter events, 29.9 us)
Async XLA Ops:
  7.2 88.8 %all-gather.3.cloned.1.call-start = ((), (), s32[]{:S(2)}) async-start(), calls=%async_computation.6 | async-start | bytes 5324800 | tf_op jit(solution)/shard_map/all_gather | solution.py:337
  8.8 3.3 %copy-start.10 = (bf16[16,1536]{1,0:T(8,128)(2,1)S(1)}, bf16[16,1536]{1,0:T(8,128)(2,1)}, u32[]{:S(2)}) copy-start(bf16[16,1536]{1,0:T(8,128)(2,1)} %param.32) | copy-start | bytes 147460
  8.8 3.2 %copy-start.11 = (bf16[16,512]{1,0:T(8,128)(2,1)S(1)}, bf16[16,512]{1,0:T(8,128)(2,1)}, u32[]{:S(2)}) copy-start(bf16[16,512]{1,0:T(8,128)(2,1)} %param.35) | copy-start | bytes 49156
  8.8 7.4 %copy-start.12 = (s32[4,144,2]{1,2,0:T(2,128)S(1)}, s32[4,144,2]{1,2,0:T(2,128)}, u32[]{:S(2)}) copy-start(s32[4,144,2]{1,2,0:T(2,128)} %param.27) | copy-start | bytes 13828
  8.8 7.5 %copy-start.15 = (s32[4]{0:T(128)S(1)}, s32[4]{0:T(128)}, u32[]{:S(2)}) copy-start(s32[4]{0:T(128)} %cnt_ref.1) | copy-start | bytes 52
  8.8 7.8 %copy-start.13 = (s32[1,576]{1,0:T(1,128)S(1)}, s32[1,576]{1,0:T(1,128)}, u32[]{:S(2)}) copy-start(s32[1,576]{1,0:T(1,128)} %param.28) | copy-start | bytes 6916
  12.2 7.9 %collective-permute-start = (bf16[1,16,2176]{2,1,0:T(8,128)(2,1)S(1)}, bf16[1,16,2176]{2,1,0:T(8,128)(2,1)S(1)}, u32[]{:S(2)}, u32[]{:S(2)}) collective-permute-start(bf16[1,16,2176]{2,1,0:T(8,128)(2,1)S(1)} %bitcast.79), channel_id=1, source_target_pairs={{0,16},{8,24},{16,0},{24,8},{1,17},{9,25},{17,1},{25,9},{2,18},{10... | collective-permute-start | bytes 208904 | tf_op jit(solution)/shard_map/ppermute | solution.py:289
  17.2 18.2 %copy-start.7 = (bf16[4,144,512]{2,1,0:T(8,128)(2,1)S(1)}, bf16[4,144,512]{2,1,0:T(8,128)(2,1)}, u32[]{:S(2)}) copy-start(bf16[4,144,512]{2,1,0:T(8,128)(2,1)} %param.29) | copy-start | bytes 1769476
  20.1 5.1 %collective-permute-start.1 = (bf16[2,16,2176]{2,1,0:T(8,128)(2,1)S(1)}, bf16[2,16,2176]{2,1,0:T(8,128)(2,1)S(1)}, u32[]{:S(2)}, u32[]{:S(2)}) collective-permute-start(bf16[2,16,2176]{2,1,0:T(8,128)(2,1)S(1)} %pad_maximum_fusion.9), channel_id=1, source_target_pairs={{0,8},{8,0},{16,24},{24,16},{1,9},{9,1},{17,25},{25,17},{2,10},{10... | collective-permute-start | bytes 417800 | tf_op jit(solution)/shard_map/ppermute | solution.py:289
  20.8 16.9 %copy-start.8 = (s32[576,2]{0,1:T(2,128)}, s32[576,2]{0,1:T(2,128)S(1)}, u32[]{:S(2)}) copy-start(s32[576,2]{0,1:T(2,128)S(1)} %and_select_fusion) | copy-start | bytes 13828
  25.2 5.3 %collective-permute-start.2 = (bf16[4,16,1024]{2,1,0:T(8,128)(2,1)S(1)}, bf16[4,16,1024]{2,1,0:T(8,128)(2,1)S(1)}, u32[]{:S(2)}, u32[]{:S(2)}) collective-permute-start(bf16[4,16,1024]{2,1,0:T(8,128)(2,1)S(1)} %pad_maximum_fusion.10), channel_id=1, source_target_pairs={{0,2},{1,3},{2,0},{3,1},{4,6},{5,7},{6,4},{7,5},{8,10},{9,11},{10,... | collective-permute-start | bytes 393224 | tf_op jit(solution)/shard_map/ppermute | solution.py:289
  27.6 6.3 %collective-permute-start.5 = (bf16[4,16,1152]{2,1,0:T(8,128)(2,1)S(1)}, bf16[4,16,1152]{2,1,0:T(8,128)(2,1)S(1)}, u32[]{:S(2)}, u32[]{:S(2)}) collective-permute-start(bf16[4,16,1152]{2,1,0:T(8,128)(2,1)S(1)} %pad_maximum_fusion.7), channel_id=1, source_target_pairs={{0,4},{1,5},{2,6},{3,7},{4,0},{5,1},{6,2},{7,3},{8,12},{9,13},{10,... | collective-permute-start | bytes 442376 | tf_op jit(solution)/shard_map/ppermute | solution.py:289
  30.5 10.8 %collective-permute-start.3 = (bf16[8,16,1024]{2,1,0:T(8,128)(2,1)S(1)}, bf16[8,16,1024]{2,1,0:T(8,128)(2,1)S(1)}, u32[]{:S(2)}, u32[]{:S(2)}) collective-permute-start(bf16[8,16,1024]{2,1,0:T(8,128)(2,1)S(1)} %pad_maximum_fusion.6), channel_id=1, source_target_pairs={{0,4},{1,5},{2,6},{3,7},{4,0},{5,1},{6,2},{7,3},{8,12},{9,13},{10,... | collective-permute-start | bytes 786440 | tf_op jit(solution)/shard_map/ppermute | solution.py:289
  33.9 8.7 %collective-permute-start.6 = (bf16[8,16,1152]{2,1,0:T(8,128)(2,1)S(1)}, bf16[8,16,1152]{2,1,0:T(8,128)(2,1)S(1)}, u32[]{:S(2)}, u32[]{:S(2)}) collective-permute-start(bf16[8,16,1152]{2,1,0:T(8,128)(2,1)S(1)} %pad_maximum_fusion.5), channel_id=1, source_target_pairs={{0,2},{1,3},{2,0},{3,1},{4,6},{5,7},{6,4},{7,5},{8,10},{9,11},{10,... | collective-permute-start | bytes 884744 | tf_op jit(solution)/shard_map/ppermute | solution.py:289
  37.7 21.0 %all-to-all-start.1 = ((bf16[8,152,512]{2,1,0:T(8,128)(2,1)}), bf16[8,152,512]{2,1,0:T(8,128)(2,1)S(1)}, u32[]{:S(2)}, u32[]{:S(2)}) async-start(bf16[8,152,512]{2,1,0:T(8,128)(2,1)} %bitcast.19), calls=%async_computation.1 | async-start | bytes 2490368 | tf_op jit(solution)/shard_map/all_to_all | solution.py:402
  42.2 3.7 %collective-permute-start.4 = (bf16[16,16,1024]{2,1,0:T(8,128)(2,1)}, bf16[16,16,1024]{2,1,0:T(8,128)(2,1)}, u32[]{:S(2)}, u32[]{:S(2)}) collective-permute-start(bf16[16,16,1024]{2,1,0:T(8,128)(2,1)} %pad_maximum_fusion.4), channel_id=1, source_target_pairs={{0,1},{1,0},{2,3},{3,2},{4,5},{5,4},{6,7},{7,6},{8,9},{9,8},{10,11... | collective-permute-start | bytes 1572872 | tf_op jit(solution)/shard_map/ppermute | solution.py:289
  42.6 5.4 %collective-permute-start.7 = (bf16[16,16,1152]{2,1,0:T(8,128)(2,1)S(1)}, bf16[16,16,1152]{2,1,0:T(8,128)(2,1)S(1)}, u32[]{:S(2)}, u32[]{:S(2)}) collective-permute-start(bf16[16,16,1152]{2,1,0:T(8,128)(2,1)S(1)} %pad_maximum_fusion.3), channel_id=1, source_target_pairs={{0,1},{1,0},{2,3},{3,2},{4,5},{5,4},{6,7},{7,6},{8,9},{9,8},{10,11... | collective-permute-start | bytes 1769480 | tf_op jit(solution)/shard_map/ppermute | solution.py:289
  59.8 37.5 %all-to-all-start = ((bf16[8,152,512]{2,1,0:T(8,128)(2,1)}), bf16[8,152,512]{2,1,0:T(8,128)(2,1)S(1)}, u32[]{:S(2)}, u32[]{:S(2)}) async-start(bf16[8,152,512]{2,1,0:T(8,128)(2,1)} %bitcast.77), calls=%async_computation | async-start | bytes 2490368 | tf_op jit(solution)/shard_map/all_to_all | solution.py:402
  63.3 161.3 %reduce-scatter.2.cloned.1.call-start = ((), (), s32[]{:S(2)}) async-start(), calls=%async_computation.5 | async-start | bytes 5324800 | tf_op jit(solution)/shard_map/reduce_scatter | solution.py:478
  153.2 3.7 %copy-start.9 = (s32[576,2]{0,1:T(2,128)S(1)}, s32[576,2]{0,1:T(2,128)}, u32[]{:S(2)}) copy-start(s32[576,2]{0,1:T(2,128)} %copy-done.8) | copy-start | bytes 13828
  153.2 21.2 %all-to-all-start.3 = ((bf16[8,152,512]{2,1,0:T(8,128)(2,1)}), bf16[8,152,512]{2,1,0:T(8,128)(2,1)S(1)}, u32[]{:S(2)}, u32[]{:S(2)}) async-start(bf16[8,152,512]{2,1,0:T(8,128)(2,1)} %bitcast.27), calls=%async_computation.3 | async-start | bytes 2490368 | tf_op jit(solution)/shard_map/all_to_all | solution.py:402
  192.6 3.2 %copy-start.6 = (bf16[32,16,1024]{2,1,0:T(8,128)(2,1)S(1)}, bf16[32,16,1024]{2,1,0:T(8,128)(2,1)}, u32[]{:S(2)}) copy-start(bf16[32,16,1024]{2,1,0:T(8,128)(2,1)} %get-tuple-element.68) | copy-start | bytes 3145732
  193.8 2.0 collective-permute-start.13
  195.0 2.2 collective-permute-start.8
  196.0 8.4 %collective-permute-start.14 = (bf16[8,16,1024]{2,1,0:T(8,128)(2,1)S(1)}, bf16[8,16,1024]{2,1,0:T(8,128)(2,1)S(1)}, u32[]{:S(2)}, u32[]{:S(2)}) collective-permute-start(bf16[8,16,1024]{2,1,0:T(8,128)(2,1)S(1)} %slice.233), channel_id=1, source_target_pairs={{0,4},{1,5},{2,6},{3,7},{4,0},{5,1},{6,2},{7,3},{8,12},{9,13},{10,... | collective-permute-start | bytes 786440 | tf_op jit(solution)/shard_map/ppermute | solution.py:289
  197.4 9.4 %collective-permute-start.9 = (bf16[8,16,1152]{2,1,0:T(8,128)(2,1)S(1)}, bf16[8,16,1152]{2,1,0:T(8,128)(2,1)S(1)}, u32[]{:S(2)}, u32[]{:S(2)}) collective-permute-start(bf16[8,16,1152]{2,1,0:T(8,128)(2,1)S(1)} %slice.223), channel_id=1, source_target_pairs={{0,2},{1,3},{2,0},{3,1},{4,6},{5,7},{6,4},{7,5},{8,10},{9,11},{10,... | collective-permute-start | bytes 884744 | tf_op jit(solution)/shard_map/ppermute | solution.py:289
  204.5 5.0 %collective-permute-start.15 = (bf16[4,16,1024]{2,1,0:T(8,128)(2,1)S(1)}, bf16[4,16,1024]{2,1,0:T(8,128)(2,1)S(1)}, u32[]{:S(2)}, u32[]{:S(2)}) collective-permute-start(bf16[4,16,1024]{2,1,0:T(8,128)(2,1)S(1)} %slice.235), channel_id=1, source_target_pairs={{0,2},{1,3},{2,0},{3,1},{4,6},{5,7},{6,4},{7,5},{8,10},{9,11},{10,... | collective-permute-start | bytes 393224 | tf_op jit(solution)/shard_map/ppermute | solution.py:289
  206.9 5.4 %collective-permute-start.10 = (bf16[4,16,1152]{2,1,0:T(8,128)(2,1)S(1)}, bf16[4,16,1152]{2,1,0:T(8,128)(2,1)S(1)}, u32[]{:S(2)}, u32[]{:S(2)}) collective-permute-start(bf16[4,16,1152]{2,1,0:T(8,128)(2,1)S(1)} %slice.225), channel_id=1, source_target_pairs={{0,4},{1,5},{2,6},{3,7},{4,0},{5,1},{6,2},{7,3},{8,12},{9,13},{10,... | collective-permute-start | bytes 442376 | tf_op jit(solution)/shard_map/ppermute | solution.py:289
  209.6 4.6 %collective-permute-start.16 = (bf16[2,16,1024]{2,1,0:T(8,128)(2,1)S(1)}, bf16[2,16,1024]{2,1,0:T(8,128)(2,1)S(1)}, u32[]{:S(2)}, u32[]{:S(2)}) collective-permute-start(bf16[2,16,1024]{2,1,0:T(8,128)(2,1)S(1)} %slice.237), channel_id=1, source_target_pairs={{0,8},{8,0},{16,24},{24,16},{1,9},{9,1},{17,25},{25,17},{2,10},{10... | collective-permute-start | bytes 196616 | tf_op jit(solution)/shard_map/ppermute | solution.py:289
  212.4 4.4 %collective-permute-start.11 = (bf16[2,16,1152]{2,1,0:T(8,128)(2,1)S(1)}, bf16[2,16,1152]{2,1,0:T(8,128)(2,1)S(1)}, u32[]{:S(2)}, u32[]{:S(2)}) collective-permute-start(bf16[2,16,1152]{2,1,0:T(8,128)(2,1)S(1)} %slice.227), channel_id=1, source_target_pairs={{0,8},{8,0},{16,24},{24,16},{1,9},{9,1},{17,25},{25,17},{2,10},{10... | collective-permute-start | bytes 221192 | tf_op jit(solution)/shard_map/ppermute | solution.py:289
  214.2 5.0 %collective-permute-start.17 = (bf16[1,16,1024]{2,1,0:T(8,128)(2,1)S(1)}, bf16[1,16,1024]{2,1,0:T(8,128)(2,1)S(1)}, u32[]{:S(2)}, u32[]{:S(2)}) collective-permute-start(bf16[1,16,1024]{2,1,0:T(8,128)(2,1)S(1)} %slice.239), channel_id=1, source_target_pairs={{0,16},{8,24},{16,0},{24,8},{1,17},{9,25},{17,1},{25,9},{2,18},{10... | collective-permute-start | bytes 98312 | tf_op jit(solution)/shard_map/ppermute | solution.py:289
  216.8 5.0 %collective-permute-start.12 = (bf16[1,16,1152]{2,1,0:T(8,128)(2,1)S(1)}, bf16[1,16,1152]{2,1,0:T(8,128)(2,1)S(1)}, u32[]{:S(2)}, u32[]{:S(2)}) collective-permute-start(bf16[1,16,1152]{2,1,0:T(8,128)(2,1)S(1)} %slice.229), channel_id=1, source_target_pairs={{0,16},{8,24},{16,0},{24,8},{1,17},{9,25},{17,1},{25,9},{2,18},{10... | collective-permute-start | bytes 110600 | tf_op jit(solution)/shard_map/ppermute | solution.py:289
  (16 other events, 36.1 us)
Sparse Core Ops, SparseCore 0:
  11.4 84.5 all-gather.2
  131.0 77.2 reduce-scatter.1
